TPU v7x, 32 devices: a whole 2x2x4 slice. The times are simulated.
32 devices in a mesh: grp: 2 (over x), row: 16 (over z, y, core).
Axes of the slice: x: 2, y: 2, z: 4, core: 2. Of those that a mesh axis runs over, the one named last changes fastest.
Arguments:
- frames: bfloat16 [4096, 8192], P('grp', 'row'), parts along dimension 0, may hold values from 0 to 1, as said below
- pattern: int32 [64, 3], P(('grp', 'row')), parts along dimension 0, may hold values from 0 to 1, as said below
- couplings: float32 [64, 3, 256, 256], P(('grp', 'row')), parts along dimension 0, may hold values from -0.7 to 0.7, as said below
- first_moment: float32 [64, 3, 256, 256], P(('grp', 'row')), parts along dimension 0, may hold values from -204.8 to 204.8, as said below
- second_moment: float32 [64, 3, 256, 256], P(('grp', 'row')), parts along dimension 0, may hold values from 0 to 104857.6, as said below
- fields: float32 [16384], P(('grp', 'row')), parts along dimension 0, may hold values from -4 to 4
- field_first: float32 [16384], P(('grp', 'row')), parts along dimension 0, may hold values from -640 to 640
- field_second: float32 [16384], P(('grp', 'row')), parts along dimension 0, may hold values from 41943.04 to 2097152
Outputs:
- new_couplings: float32 [64, 3, 256, 256], P(('grp', 'row')), parts along dimension 0
- new_first: float32 [64, 3, 256, 256], P(('grp', 'row')), parts along dimension 0
- new_second: float32 [64, 3, 256, 256], P(('grp', 'row')), parts along dimension 0
- new_fields: float32 [16384], P(('grp', 'row')), parts along dimension 0
- new_field_first: float32 [16384], P(('grp', 'row')), parts along dimension 0
- new_field_second: float32 [16384], P(('grp', 'row')), parts along dimension 0
There are 2 independent parts, one for each index of `grp`. A program takes and returns all parts, laid end to end along the dimension named above; each array names one. Nothing has to cross between parts.
Inputs may be any that keep to these rules, and one draw needn't show every extreme that they name: Entries are 0 or 1. Column 1 is always 1; pattern[b, 2] equals pattern[b + 1, 0]; pattern[0, 0] and pattern[31, 2] are 0. `frames`: 0 or 1. `couplings`: zero in every block whose pattern entry is 0 and on the diagonal of slot 1; slot 1 of each block row is symmetric; slot 0 of block row b is the transpose of slot 2 of block row b - 1. `first_moment`: same zeros and mirror structure as couplings. `second_moment`: same zeros and mirror structure as couplings; not negative.
All inputs are finite; a program needn't handle non-finite values.
Results may differ from a plain program's by a relative error of at most 0.0012.
Values may be sent and summed in bfloat16 or wider, within the bound.
A program may use at most 64 MiB of HBM per device.

v0:
```python
import jax
import jax.numpy as jnp
from jax import lax
from jax.sharding import PartitionSpec as P

STEPS = 2
PRIOR_STEPS = 100


BETA_ONE = 0.9
BETA_TWO = 0.999
LEARN_RATE = 0.02
EPSILON = 1e-08


def with_halo(block, sides, width):
    for axis, dim in sides:
        count = lax.axis_size(axis)
        forward = [(i, i + 1) for i in range(count - 1)]
        backward = [(target, source) for source, target in forward]
        low = lax.ppermute(
            lax.slice_in_dim(block, block.shape[dim] - width, None, axis=dim), axis, forward
        )
        high = lax.ppermute(lax.slice_in_dim(block, 0, width, axis=dim), axis, backward)
        block = jnp.concatenate([low, block, high], axis=dim)
    return block


def adam_update(parameter, first_moment, second_moment, gradient, step_count):
    first_moment = BETA_ONE * first_moment + (1.0 - BETA_ONE) * gradient
    second_moment = BETA_TWO * second_moment + (1.0 - BETA_TWO) * gradient * gradient
    first_hat = first_moment / (1.0 - BETA_ONE**step_count)
    second_hat = second_moment / (1.0 - BETA_TWO**step_count)
    parameter = parameter - LEARN_RATE * first_hat / (jnp.sqrt(second_hat) + EPSILON)
    return (parameter, first_moment, second_moment)


def on_device(
    frames, pattern, couplings, first_moment, second_moment, fields, field_first, field_second
):
    frame_count = frames.shape[0]
    block_width = couplings.shape[-1]
    spikes = frames.reshape(frame_count, 2, block_width)
    spikes_float = spikes.astype(jnp.float32)
    occupied = pattern.astype(jnp.float32)
    all_ones = jnp.ones((block_width, block_width), jnp.float32)
    identity_matrix = jnp.eye(block_width, dtype=jnp.float32)
    slot_mask = (
        occupied[:, :, None, None]
        * jnp.stack([all_ones, all_ones - identity_matrix, all_ones])[None]
    )
    field_rows = fields.reshape(2, block_width)
    for step_index in range(STEPS):
        step_count = PRIOR_STEPS + step_index + 1
        weights = couplings.astype(jnp.bfloat16)
        logit_terms = jnp.einsum(
            "frb,rsbc->rsfc", spikes, weights, preferred_element_type=jnp.float32
        )
        rim_values = with_halo(
            jnp.stack([logit_terms[0, 0], logit_terms[1, 2]]).astype(jnp.bfloat16), (("row", 0),), 1
        ).astype(jnp.float32)
        from_below, from_above = (rim_values[0], rim_values[3])
        logit_low = field_rows[0] + logit_terms[0, 1] + logit_terms[1, 0] + from_below
        logit_high = field_rows[1] + logit_terms[1, 1] + logit_terms[0, 2] + from_above
        logits = jnp.stack([logit_low, logit_high], axis=1)
        deviation = jax.nn.sigmoid(logits) - spikes_float
        residual = deviation.astype(jnp.bfloat16).reshape(frame_count, 2 * block_width)
        field_grad = jnp.sum(deviation, axis=0).reshape(2 * block_width)
        extended = with_halo(residual, (("row", 1),), block_width)
        windows = extended.reshape(frame_count, 4, block_width)
        halves = jnp.stack(
            [
                jnp.einsum(
                    "fb,fsc->sbc",
                    spikes[:, local_row],
                    windows[:, local_row : local_row + 3],
                    preferred_element_type=jnp.float32,
                )
                for local_row in range(2)
            ]
        )
        mirror_values = with_halo(
            jnp.stack([halves[0, 0], halves[1, 2]]).astype(jnp.bfloat16), (("row", 0),), 1
        ).astype(jnp.float32)
        mirror_below, mirror_above = (mirror_values[0], mirror_values[3])
        grad_low = jnp.stack(
            [
                halves[0, 0] + mirror_below.T,
                halves[0, 1] + halves[0, 1].T,
                halves[0, 2] + halves[1, 0].T,
            ]
        )
        grad_high = jnp.stack(
            [
                halves[1, 0] + halves[0, 2].T,
                halves[1, 1] + halves[1, 1].T,
                halves[1, 2] + mirror_above.T,
            ]
        )
        gradient = jnp.stack([grad_low, grad_high]) * slot_mask
        couplings, first_moment, second_moment = adam_update(
            couplings, first_moment, second_moment, gradient, step_count
        )
        fields, field_first, field_second = adam_update(
            fields, field_first, field_second, field_grad, step_count
        )
        field_rows = fields.reshape(2, block_width)
    return (couplings, first_moment, second_moment, fields, field_first, field_second)


def solution(mesh):
    in_specs = (
        P("grp", "row"),
        P(("grp", "row"), None),
        P(("grp", "row"), None, None, None),
        P(("grp", "row"), None, None, None),
        P(("grp", "row"), None, None, None),
        P(("grp", "row")),
        P(("grp", "row")),
        P(("grp", "row")),
    )
    out_specs = (
        P(("grp", "row"), None, None, None),
        P(("grp", "row"), None, None, None),
        P(("grp", "row"), None, None, None),
        P(("grp", "row")),
        P(("grp", "row")),
        P(("grp", "row")),
    )
    return jax.shard_map(
        on_device, mesh=mesh, in_specs=in_specs, out_specs=out_specs, check_vma=False
    )
```

profile of v0, /device:TPU:1, one launch (start us, length us, event | category | flops | bytes accessed | tf_op | source)
XLA Modules:
  0.0 222.3 jit_solution(9262997408299292529)
XLA Ops:
  0.6 2.9 %copy.35 = bf16[2048,512]{0,1:T(8,128)(2,1)S(1)} copy(bf16[2048,512]{1,0:T(8,128)(2,1)} %param.8) | data formatting | bytes 4194304 | tf_op args[0]
  3.6 4.0 %fusion.55 = (bf16[2,3,2048,256]{2,3,1,0:T(8,128)(2,1)S(1)}, f32[2,3,2048,256]{2,3,1,0:T(8,128)S(1)}) fusion(bf16[2048,2,256,1]{0,2,3,1:T(8,128)(2,1)S(1)} %bitcast.257, f32[2,3,256,256]{3,2,1,0:T(8,128)} %param.10), kind=kOutput, calls=%fused_computation.132 | convolution fusion | flops 1614151680 | bytes 22544384 | tf_op jit(solution)/shard_map/frb,rsbc->rsfc/dot_general | solution.py:56
  7.9 4.5 %collective-permute-start = (bf16[1,2048,256]{1,2,0:T(8,128)(2,1)S(1)}, bf16[1,2048,256]{1,2,0:T(8,128)(2,1)S(1)}, u32[]{:S(2)}, u32[]{:S(2)}) collective-permute-start(bf16[1,2048,256]{1,2,0:T(8,128)(2,1)S(1)} %get-tuple-element.22), channel_id=1, source_target_pairs={{0,1},{1,2},{2,3},{3,4},{4,5},{5,6},{6,7},{7,8},{8,9},{9,10},{10,1... | collective-permute-start | bytes 3145736 | tf_op jit(solution)/shard_map/ppermute | solution.py:21
  14.4 21.0 %collective-permute-done = bf16[1,2048,256]{1,2,0:T(8,128)(2,1)S(1)} collective-permute-done((bf16[1,2048,256]{1,2,0:T(8,128)(2,1)S(1)}, bf16[1,2048,256]{1,2,0:T(8,128)(2,1)S(1)}, u32[]{:S(2)}, u32[]{:S(2)}) %collective-permute-start) | collective-permute-done | bytes 1048608 | tf_op jit(solution)/shard_map/ppermute | solution.py:21
  36.5 3.1 %fusion.2 = f32[2048,2,256]{0,2,1:T(8,128)} fusion(f32[2048,1,256]{0,2,1:T(8,128)S(1)} %get-tuple-element.15, f32[2048,1,256]{0,2,1:T(8,128)S(1)} %get-tuple-element.14), kind=kLoop, calls=%fused_computation.7 | loop fusion | flops 4194304 | bytes 8388608 | tf_op jit(solution)/shard_map/div | solution.py:66
  39.6 5.6 %copy.38 = f32[2048,512]{1,0:T(8,128)} copy(f32[2048,512]{0,1:T(8,128)} %bitcast.263) | data formatting | bytes 8388608 | tf_op jit(solution)/shard_map/div | solution.py:66
  45.2 3.0 %fusion.6 = (f32[512]{0:T(512)S(1)}, bf16[2048,512]{1,0:T(8,128)(2,1)S(1)}) fusion(f32[2048,512]{1,0:T(8,128)} %copy.38, bf16[2048,512]{1,0:T(8,128)(2,1)S(1)} %copy-done), kind=kLoop, calls=%fused_computation.14 | loop fusion | flops 4193792 | bytes 8390656 | tf_op jit(solution)/shard_map/reduce_sum | solution.py:68
  48.3 4.4 %collective-permute-start.2 = (bf16[2048,256]{1,0:T(8,128)(2,1)S(1)}, bf16[2048,256]{1,0:T(8,128)(2,1)S(1)}, u32[]{:S(2)}, u32[]{:S(2)}) collective-permute-start(bf16[2048,256]{1,0:T(8,128)(2,1)S(1)} %get-tuple-element.26), channel_id=1, source_target_pairs={{0,1},{1,2},{2,3},{3,4},{4,5},{5,6},{6,7},{7,8},{8,9},{9,10},{10,1... | collective-permute-start | bytes 3145736 | tf_op jit(solution)/shard_map/ppermute | solution.py:21
  54.8 20.9 %collective-permute-done.2 = bf16[2048,256]{1,0:T(8,128)(2,1)S(1)} collective-permute-done((bf16[2048,256]{1,0:T(8,128)(2,1)S(1)}, bf16[2048,256]{1,0:T(8,128)(2,1)S(1)}, u32[]{:S(2)}, u32[]{:S(2)}) %collective-permute-start.2) | collective-permute-done | bytes 1048608 | tf_op jit(solution)/shard_map/ppermute | solution.py:21
  77.9 6.5 %copy.39 = bf16[2048,1024]{0,1:T(8,128)(2,1)} copy(bf16[2048,1024]{1,0:T(8,128)(2,1)} %pad_maximum_fusion) | data formatting | bytes 8388608 | tf_op jit(solution)/shard_map/concatenate | solution.py:25
  84.5 3.3 %convolution_bitcast_fusion.4 = f32[1,3,256,256]{2,3,1,0:T(8,128)S(1)} fusion(bf16[2048,4,256]{0,2,1:T(8,128)(2,1)} %bitcast.267, bf16[2048,2,256]{0,2,1:T(8,128)(2,1)} %bitcast.258), kind=kOutput, calls=%fused_computation.52 | convolution fusion | flops 805306368 | bytes 6029312 | tf_op jit(solution)/shard_map/fb,fsc->sbc/dot_general | solution.py:73
  92.6 4.4 %collective-permute-start.4 = (bf16[1,256,256]{1,2,0:T(8,128)(2,1)}, bf16[1,256,256]{1,2,0:T(8,128)(2,1)}, u32[]{:S(2)}, u32[]{:S(2)}) collective-permute-start(bf16[1,256,256]{1,2,0:T(8,128)(2,1)} %fusion.43), channel_id=1, source_target_pairs={{0,1},{1,2},{2,3},{3,4},{4,5},{5,6},{6,7},{7,8},{8,9},{9,10},{10,1... | collective-permute-start | bytes 393224 | tf_op jit(solution)/shard_map/ppermute | solution.py:21
  120.0 2.8 %divide_subtract_fusion.1 = f32[2,3,256,256]{3,2,1,0:T(8,128)S(1)} fusion(f32[2,3,256,256]{3,2,1,0:T(8,128)} %param.10, f32[3,256,256]{2,1,0:T(8,128)S(1)} %pad_maximum_fusion.8, f32[2,3]{1,0:T(2,128)S(1)} %convert_element_type.55, f32[1,3,256,256]{3,2,1,0:T(8,128)S(1)} %get-tuple-element.53, f32[1,3,256,256]{3,2,1,0:T(8,128)S(1)} %get-tuple-element.52, ...), kind=kLoop, calls=%fused_computation.48 | loop fusion | flops 5898240 | bytes 8650776 | tf_op jit(solution)/shard_map/sub | solution.py:34
  124.9 3.6 %collective-permute-start.6 = (bf16[1,2048,256]{1,2,0:T(8,128)(2,1)S(1)}, bf16[1,2048,256]{1,2,0:T(8,128)(2,1)S(1)}, u32[]{:S(2)}, u32[]{:S(2)}) collective-permute-start(bf16[1,2048,256]{1,2,0:T(8,128)(2,1)S(1)} %get-tuple-element.20), channel_id=1, source_target_pairs={{0,1},{1,2},{2,3},{3,4},{4,5},{5,6},{6,7},{7,8},{8,9},{9,10},{10,1... | collective-permute-start | bytes 3145736 | tf_op jit(solution)/shard_map/ppermute | solution.py:21
  130.5 21.0 %collective-permute-done.6 = bf16[1,2048,256]{1,2,0:T(8,128)(2,1)S(1)} collective-permute-done((bf16[1,2048,256]{1,2,0:T(8,128)(2,1)S(1)}, bf16[1,2048,256]{1,2,0:T(8,128)(2,1)S(1)}, u32[]{:S(2)}, u32[]{:S(2)}) %collective-permute-start.6) | collective-permute-done | bytes 1048608 | tf_op jit(solution)/shard_map/ppermute | solution.py:21
  152.7 3.1 %fusion.5 = f32[2048,2,256]{0,2,1:T(8,128)} fusion(f32[2048,1,256]{0,2,1:T(8,128)S(1)} %get-tuple-element.13, f32[2048,1,256]{0,2,1:T(8,128)S(1)} %get-tuple-element.12), kind=kLoop, calls=%fused_computation.12 | loop fusion | flops 4194304 | bytes 8388608 | tf_op jit(solution)/shard_map/div | solution.py:66
  155.7 5.4 %copy.52 = f32[2048,512]{1,0:T(8,128)} copy(f32[2048,512]{0,1:T(8,128)} %bitcast.264) | data formatting | bytes 8388608 | tf_op jit(solution)/shard_map/div | solution.py:66
  161.1 3.0 %fusion.8 = (f32[512]{0:T(512)S(1)}, bf16[2048,512]{1,0:T(8,128)(2,1)S(1)}) fusion(f32[2048,512]{1,0:T(8,128)} %copy.52, bf16[2048,512]{1,0:T(8,128)(2,1)S(1)} %copy-done), kind=kLoop, calls=%fused_computation.16 | loop fusion | flops 4193792 | bytes 8390656 | tf_op jit(solution)/shard_map/reduce_sum | solution.py:68
  164.3 4.4 %collective-permute-start.8 = (bf16[2048,256]{1,0:T(8,128)(2,1)S(1)}, bf16[2048,256]{1,0:T(8,128)(2,1)S(1)}, u32[]{:S(2)}, u32[]{:S(2)}) collective-permute-start(bf16[2048,256]{1,0:T(8,128)(2,1)S(1)} %get-tuple-element.24), channel_id=1, source_target_pairs={{0,1},{1,2},{2,3},{3,4},{4,5},{5,6},{6,7},{7,8},{8,9},{9,10},{10,1... | collective-permute-start | bytes 3145736 | tf_op jit(solution)/shard_map/ppermute | solution.py:21
  171.2 20.4 %collective-permute-done.8 = bf16[2048,256]{1,0:T(8,128)(2,1)S(1)} collective-permute-done((bf16[2048,256]{1,0:T(8,128)(2,1)S(1)}, bf16[2048,256]{1,0:T(8,128)(2,1)S(1)}, u32[]{:S(2)}, u32[]{:S(2)}) %collective-permute-start.8) | collective-permute-done | bytes 1048608 | tf_op jit(solution)/shard_map/ppermute | solution.py:21
  193.9 6.6 %copy.53 = bf16[2048,1024]{0,1:T(8,128)(2,1)} copy(bf16[2048,1024]{1,0:T(8,128)(2,1)} %pad_maximum_fusion.1) | data formatting | bytes 8388608 | tf_op jit(solution)/shard_map/concatenate | solution.py:25
  200.6 3.1 %convolution_bitcast_fusion.3 = f32[1,3,256,256]{3,2,1,0:T(8,128)S(1)} fusion(bf16[2048,4,256]{0,2,1:T(8,128)(2,1)} %bitcast.265, bf16[2048,2,256]{0,2,1:T(8,128)(2,1)S(1)} %bitcast.261), kind=kOutput, calls=%fused_computation.51 | convolution fusion | flops 805306368 | bytes 6029312 | tf_op jit(solution)/shard_map/fb,fsc->sbc/dot_general | solution.py:73
  207.7 4.6 %collective-permute-start.10 = (bf16[1,256,256]{2,1,0:T(8,128)(2,1)S(1)}, bf16[1,256,256]{2,1,0:T(8,128)(2,1)S(1)}, u32[]{:S(2)}, u32[]{:S(2)}) collective-permute-start(bf16[1,256,256]{2,1,0:T(8,128)(2,1)S(1)} %fusion.45), channel_id=1, source_target_pairs={{0,1},{1,2},{2,3},{3,4},{4,5},{5,6},{6,7},{7,8},{8,9},{9,10},{10,1... | collective-permute-start | bytes 393224 | tf_op jit(solution)/shard_map/ppermute | solution.py:21
  219.0 3.4 %divide_subtract_fusion = (f32[2,3,256,256]{3,2,1,0:T(8,128)}, f32[2,3,256,256]{3,2,1,0:T(8,128)}, f32[2,3,256,256]{3,2,1,0:T(8,128)}) fusion(f32[2,3,256,256]{3,2,1,0:T(8,128)S(1)} %copy-done.6, f32[1,3,256,256]{3,2,1,0:T(8,128)S(1)} %maximum_bitcast_fusion.3, f32[1,3,256,256]{3,2,1,0:T(8,128)S(1)} %maximum_bitcast_fusion.2, ...), kind=kLoop, calls=%fused_computation.46 | loop fusion | flops 9437184 | bytes 13369368 | tf_op jit(solution)/shard_map/sub | solution.py:34
  (122 shorter events, 56.2 us)
Async XLA Ops:
  3.6 4.0 %copy-start.1 = (bf16[2048,512]{0,1:T(8,128)(2,1)}, bf16[2048,512]{0,1:T(8,128)(2,1)S(1)}, u32[]{:S(2)}) copy-start(bf16[2048,512]{0,1:T(8,128)(2,1)S(1)} %copy.35) | copy-start | bytes 6291460
  7.6 6.7 %copy-start.24 = (f32[512]{0:T(512)S(1)}, f32[512]{0:T(512)}, u32[]{:S(2)}) copy-start(f32[512]{0:T(512)} %param.13) | copy-start | bytes 6148
  7.9 27.5 %collective-permute-start = (bf16[1,2048,256]{1,2,0:T(8,128)(2,1)S(1)}, bf16[1,2048,256]{1,2,0:T(8,128)(2,1)S(1)}, u32[]{:S(2)}, u32[]{:S(2)}) collective-permute-start(bf16[1,2048,256]{1,2,0:T(8,128)(2,1)S(1)} %get-tuple-element.22), channel_id=1, source_target_pairs={{0,1},{1,2},{2,3},{3,4},{4,5},{5,6},{6,7},{7,8},{8,9},{9,10},{10,1... | collective-permute-start | bytes 3145736 | tf_op jit(solution)/shard_map/ppermute | solution.py:21
  12.4 23.0 %collective-permute-start.1 = (bf16[1,2048,256]{1,2,0:T(8,128)(2,1)S(1)}, bf16[1,2048,256]{1,2,0:T(8,128)(2,1)S(1)}, u32[]{:S(2)}, u32[]{:S(2)}) collective-permute-start(bf16[1,2048,256]{1,2,0:T(8,128)(2,1)S(1)} %get-tuple-element.23), channel_id=1, source_target_pairs={{1,0},{2,1},{3,2},{4,3},{5,4},{6,5},{7,6},{8,7},{9,8},{10,9},{11,1... | collective-permute-start | bytes 3145736 | tf_op jit(solution)/shard_map/ppermute | solution.py:24
  39.6 5.6 %copy-start = (bf16[2048,512]{1,0:T(8,128)(2,1)S(1)}, bf16[2048,512]{1,0:T(8,128)(2,1)}, u32[]{:S(2)}) copy-start(bf16[2048,512]{1,0:T(8,128)(2,1)} %param.8) | copy-start | bytes 6291460
  48.1 6.5 %copy-start.27 = (s32[2,3]{1,0:T(2,128)S(1)}, s32[2,3]{1,0:T(2,128)}, u32[]{:S(2)}) copy-start(s32[2,3]{1,0:T(2,128)} %param.9) | copy-start | bytes 76
  48.3 27.4 %collective-permute-start.2 = (bf16[2048,256]{1,0:T(8,128)(2,1)S(1)}, bf16[2048,256]{1,0:T(8,128)(2,1)S(1)}, u32[]{:S(2)}, u32[]{:S(2)}) collective-permute-start(bf16[2048,256]{1,0:T(8,128)(2,1)S(1)} %get-tuple-element.26), channel_id=1, source_target_pairs={{0,1},{1,2},{2,3},{3,4},{4,5},{5,6},{6,7},{7,8},{8,9},{9,10},{10,1... | collective-permute-start | bytes 3145736 | tf_op jit(solution)/shard_map/ppermute | solution.py:21
  52.7 23.0 %collective-permute-start.3 = (bf16[2048,256]{1,0:T(8,128)(2,1)S(1)}, bf16[2048,256]{1,0:T(8,128)(2,1)S(1)}, u32[]{:S(2)}, u32[]{:S(2)}) collective-permute-start(bf16[2048,256]{1,0:T(8,128)(2,1)S(1)} %get-tuple-element.27), channel_id=1, source_target_pairs={{1,0},{2,1},{3,2},{4,3},{5,4},{6,5},{7,6},{8,7},{9,8},{10,9},{11,1... | collective-permute-start | bytes 3145736 | tf_op jit(solution)/shard_map/ppermute | solution.py:24
  84.5 3.4 %copy-start.2 = (bf16[2048,512]{0,1:T(8,128)(2,1)S(1)}, bf16[2048,512]{0,1:T(8,128)(2,1)}, u32[]{:S(2)}) copy-start(bf16[2048,512]{0,1:T(8,128)(2,1)} %copy-done.1) | copy-start | bytes 6291460
  84.5 4.1 %copy-start.16 = (bf16[2048,1024]{0,1:T(8,128)(2,1)S(1)}, bf16[2048,1024]{0,1:T(8,128)(2,1)}, u32[]{:S(2)}) copy-start(bf16[2048,1024]{0,1:T(8,128)(2,1)} %copy.39) | copy-start | bytes 12582916
  88.5 3.3 %copy-start.18 = (f32[1,3,256,256]{2,3,1,0:T(8,128)}, f32[1,3,256,256]{2,3,1,0:T(8,128)S(1)}, u32[]{:S(2)}) copy-start(f32[1,3,256,256]{2,3,1,0:T(8,128)S(1)} %convolution_bitcast_fusion.4) | copy-start | bytes 2359300
  92.6 14.7 %collective-permute-start.4 = (bf16[1,256,256]{1,2,0:T(8,128)(2,1)}, bf16[1,256,256]{1,2,0:T(8,128)(2,1)}, u32[]{:S(2)}, u32[]{:S(2)}) collective-permute-start(bf16[1,256,256]{1,2,0:T(8,128)(2,1)} %fusion.43), channel_id=1, source_target_pairs={{0,1},{1,2},{2,3},{3,4},{4,5},{5,6},{6,7},{7,8},{8,9},{9,10},{10,1... | collective-permute-start | bytes 393224 | tf_op jit(solution)/shard_map/ppermute | solution.py:21
  97.0 10.3 %collective-permute-start.5 = (bf16[1,256,256]{1,2,0:T(8,128)(2,1)S(1)}, bf16[1,256,256]{1,2,0:T(8,128)(2,1)}, u32[]{:S(2)}, u32[]{:S(2)}) collective-permute-start(bf16[1,256,256]{1,2,0:T(8,128)(2,1)S(1)} %fusion.42), channel_id=1, source_target_pairs={{1,0},{2,1},{3,2},{4,3},{5,4},{6,5},{7,6},{8,7},{9,8},{10,9},{11,1... | collective-permute-start | bytes 393224 | tf_op jit(solution)/shard_map/ppermute | solution.py:24
  110.5 6.8 %copy-start.22 = (f32[1,256,256]{2,1,0:T(8,128)S(1)}, f32[1,256,256]{2,1,0:T(8,128)}, u32[]{:S(2)}) copy-start(f32[1,256,256]{2,1,0:T(8,128)} %fusion.37) | copy-start | bytes 786436
  124.6 5.9 %copy-start.25 = (f32[512]{0:T(512)S(1)}, f32[512]{0:T(512)}, u32[]{:S(2)}) copy-start(f32[512]{0:T(512)} %param.14) | copy-start | bytes 6148
  124.6 5.8 %copy-start.26 = (f32[512]{0:T(512)S(1)}, f32[512]{0:T(512)}, u32[]{:S(2)}) copy-start(f32[512]{0:T(512)} %param.15) | copy-start | bytes 6148
  124.9 26.6 %collective-permute-start.6 = (bf16[1,2048,256]{1,2,0:T(8,128)(2,1)S(1)}, bf16[1,2048,256]{1,2,0:T(8,128)(2,1)S(1)}, u32[]{:S(2)}, u32[]{:S(2)}) collective-permute-start(bf16[1,2048,256]{1,2,0:T(8,128)(2,1)S(1)} %get-tuple-element.20), channel_id=1, source_target_pairs={{0,1},{1,2},{2,3},{3,4},{4,5},{5,6},{6,7},{7,8},{8,9},{9,10},{10,1... | collective-permute-start | bytes 3145736 | tf_op jit(solution)/shard_map/ppermute | solution.py:21
  128.5 23.0 %collective-permute-start.7 = (bf16[1,2048,256]{1,2,0:T(8,128)(2,1)S(1)}, bf16[1,2048,256]{1,2,0:T(8,128)(2,1)S(1)}, u32[]{:S(2)}, u32[]{:S(2)}) collective-permute-start(bf16[1,2048,256]{1,2,0:T(8,128)(2,1)S(1)} %get-tuple-element.21), channel_id=1, source_target_pairs={{1,0},{2,1},{3,2},{4,3},{5,4},{6,5},{7,6},{8,7},{9,8},{10,9},{11,1... | collective-permute-start | bytes 3145736 | tf_op jit(solution)/shard_map/ppermute | solution.py:24
  164.3 27.4 %collective-permute-start.8 = (bf16[2048,256]{1,0:T(8,128)(2,1)S(1)}, bf16[2048,256]{1,0:T(8,128)(2,1)S(1)}, u32[]{:S(2)}, u32[]{:S(2)}) collective-permute-start(bf16[2048,256]{1,0:T(8,128)(2,1)S(1)} %get-tuple-element.24), channel_id=1, source_target_pairs={{0,1},{1,2},{2,3},{3,4},{4,5},{5,6},{6,7},{7,8},{8,9},{9,10},{10,1... | collective-permute-start | bytes 3145736 | tf_op jit(solution)/shard_map/ppermute | solution.py:21
  168.7 23.0 %collective-permute-start.9 = (bf16[2048,256]{1,0:T(8,128)(2,1)S(1)}, bf16[2048,256]{1,0:T(8,128)(2,1)S(1)}, u32[]{:S(2)}, u32[]{:S(2)}) collective-permute-start(bf16[2048,256]{1,0:T(8,128)(2,1)S(1)} %get-tuple-element.25), channel_id=1, source_target_pairs={{1,0},{2,1},{3,2},{4,3},{5,4},{6,5},{7,6},{8,7},{9,8},{10,9},{11,1... | collective-permute-start | bytes 3145736 | tf_op jit(solution)/shard_map/ppermute | solution.py:24
  193.9 6.6 %copy-start.4 = (bf16[2048,512]{0,1:T(8,128)(2,1)S(1)}, bf16[2048,512]{0,1:T(8,128)(2,1)}, u32[]{:S(2)}) copy-start(bf16[2048,512]{0,1:T(8,128)(2,1)} %copy-done.1) | copy-start | bytes 6291460
  204.9 8.4 %copy-start.20 = (f32[1,3,256,256]{3,2,1,0:T(8,128)S(1)}, f32[1,3,256,256]{3,2,1,0:T(8,128)}, u32[]{:S(2)}) copy-start(f32[1,3,256,256]{3,2,1,0:T(8,128)} %copy-done.19) | copy-start | bytes 2359300
  205.8 9.2 %collective-permute-start.11 = (bf16[1,256,256]{2,1,0:T(8,128)(2,1)S(1)}, bf16[1,256,256]{2,1,0:T(8,128)(2,1)S(1)}, u32[]{:S(2)}, u32[]{:S(2)}) collective-permute-start(bf16[1,256,256]{2,1,0:T(8,128)(2,1)S(1)} %fusion.44), channel_id=1, source_target_pairs={{1,0},{2,1},{3,2},{4,3},{5,4},{6,5},{7,6},{8,7},{9,8},{10,9},{11,1... | collective-permute-start | bytes 393224 | tf_op jit(solution)/shard_map/ppermute | solution.py:24
  207.7 7.3 %collective-permute-start.10 = (bf16[1,256,256]{2,1,0:T(8,128)(2,1)S(1)}, bf16[1,256,256]{2,1,0:T(8,128)(2,1)S(1)}, u32[]{:S(2)}, u32[]{:S(2)}) collective-permute-start(bf16[1,256,256]{2,1,0:T(8,128)(2,1)S(1)} %fusion.45), channel_id=1, source_target_pairs={{0,1},{1,2},{2,3},{3,4},{4,5},{5,6},{6,7},{7,8},{8,9},{9,10},{10,1... | collective-permute-start | bytes 393224 | tf_op jit(solution)/shard_map/ppermute | solution.py:21
  (16 other events, 29.1 us)
where the time goes:
time: 224 us; the launch traced here: 222 us
  waiting for transfers between devices  83.3 us (37%)
  local copies, waits for them, and re-layouts  48.8 us (22%)
  starting transfers between devices  37.6 us (17%)
  other arithmetic  36.9 us (16%)
  matrix products  14.4 us (6%)
    ppermute x6, waiting for transfers between devices, with_halo(): lax.ppermute(lax.slice_in_dim(block, block.shape[dim] - width, None, axis...  83.3 us
    ppermute x6, starting transfers between devices, with_halo(): lax.ppermute(lax.slice_in_dim(block, block.shape[dim] - width, None, axis...  25.9 us
    concatenate x4, local copies, waits for them, and re-layouts, with_halo(): block = jnp.concatenate([low, block, high], axis=dim)  14.6 us
    ppermute x6, starting transfers between devices, with_halo(): lax.ppermute(lax.slice_in_dim(block, 0, width, axis=dim), axis, backward)  11.7 us
    div x2, local copies, waits for them, and re-layouts, on_device(): deviation = jax.nn.sigmoid(logits) - spikes_float  11 us
    dot_general x4, matrix products, on_device(): jnp.einsum('fb,fsc->sbc', spikes[:, local_row], windows[:, local_row:loca...  8.54 us
    unnamed x57, local copies, waits for them, and re-layouts  8.46 us
    another operation x4, other arithmetic, on_device(): jnp.stack([halves[0, 0] + mirror_below.T, halves[0, 1] + halves[0, 1].T,...  7.36 us
  transfers between devices with their start and end apart: 12, of which 4 were waited for; matrix products, arithmetic and copies ran while one was open for 5% of the time, Pallas kernels for 0%

commit v1 on v0

v1 whole, which is shorter than its diff:
```python
import functools

import jax
import jax.numpy as jnp
from jax import lax
from jax.experimental import pallas as pl
from jax.experimental.pallas import tpu as pltpu
from jax.sharding import PartitionSpec as P

PRIOR_STEPS = 100
BETA_ONE = 0.9
BETA_TWO = 0.999
LEARN_RATE = 0.02
EPSILON = 1e-08
MESH = pl.DeviceIdType.MESH
PIECE = 256
SPAN = 512


def adam_update(parameter, first_moment, second_moment, gradient, step_count):
    first_moment = BETA_ONE * first_moment + (1.0 - BETA_ONE) * gradient
    second_moment = BETA_TWO * second_moment + (1.0 - BETA_TWO) * gradient * gradient
    first_rate = LEARN_RATE / (1.0 - BETA_ONE**step_count)
    second_hat = second_moment * (1.0 / (1.0 - BETA_TWO**step_count))
    parameter = parameter - first_rate * first_moment / (jnp.sqrt(second_hat) + EPSILON)
    return (parameter, first_moment, second_moment)


def dot(a, b):
    return jnp.dot(a, b, preferred_element_type=jnp.float32)


def dot_nt(a, b):
    return lax.dot_general(a, b, (((1,), (1,)), ((), ())), preferred_element_type=jnp.float32)


def kernel(
    count,
    frames_hbm, pattern, p_hbm, m_hbm, v_hbm, fields, field_first, field_second,
    p_out, m_out, v_out, grad_out, fields_out, field_first_out, field_second_out, field_grad_out,
    own, low, high, turned, p, m, v, w_own, w_low, w_high, half_low, half_high, field_sum,
    mirror_send, mirror_recv,
    halo_send_sem, halo_recv_sem, mirror_send_sem, mirror_recv_sem, own_sem, pmv_sem, out_sem,
):
    frame_count, width = low.shape
    pieces = frame_count // PIECE
    me = lax.axis_index("row")
    left = lax.rem(me + count - 1, count)
    right = lax.rem(me + 1, count)
    has_left = me > 0
    has_right = me < count - 1

    own_copy = pltpu.make_async_copy(frames_hbm, own, own_sem)
    pmv_copies = [
        pltpu.make_async_copy(src, dst, pmv_sem.at[k])
        for k, (src, dst) in enumerate(((p_hbm, p), (m_hbm, m), (v_hbm, v)))
    ]
    own_copy.start()
    for c in pmv_copies:
        c.start()

    def halo_copy(flow, i):
        rows = pl.ds(pl.multiple_of(i * PIECE, PIECE), PIECE)
        return pltpu.make_async_remote_copy(
            src_ref=frames_hbm.at[rows, pl.ds(flow * width, width)],
            dst_ref=(high, low)[flow].at[rows, :],
            send_sem=halo_send_sem.at[flow, i],
            recv_sem=halo_recv_sem.at[flow, i],
            device_id={"row": (left, right)[flow]},
            device_id_type=MESH,
        )

    def mirror_copy(step, flow):
        return pltpu.make_async_remote_copy(
            src_ref=mirror_send.at[step, flow],
            dst_ref=mirror_recv.at[step, flow],
            send_sem=mirror_send_sem.at[step, flow],
            recv_sem=mirror_recv_sem.at[step, flow],
            device_id={"row": (left, right)[flow]},
            device_id_type=MESH,
        )

    barrier = pltpu.get_barrier_semaphore()

    @pl.when(has_left)
    def _():
        pl.semaphore_signal(barrier, inc=1, device_id={"row": left}, device_id_type=MESH)

    @pl.when(has_right)
    def _():
        pl.semaphore_signal(barrier, inc=1, device_id={"row": right}, device_id_type=MESH)

    pl.semaphore_wait(barrier, has_left.astype(jnp.int32) + has_right.astype(jnp.int32))

    @pl.loop(0, pieces)
    def _(i):
        @pl.when(has_left)
        def _():
            halo_copy(0, i).start()

        @pl.when(has_right)
        def _():
            halo_copy(1, i).start()

    @pl.when(jnp.logical_not(has_left))
    def _():
        low[...] = jnp.zeros_like(low)
        for step in range(2):
            mirror_recv[step, 1] = jnp.zeros((width, width), jnp.bfloat16)

    @pl.when(jnp.logical_not(has_right))
    def _():
        high[...] = jnp.zeros_like(high)
        for step in range(2):
            mirror_recv[step, 0] = jnp.zeros((width, width), jnp.bfloat16)

    diagonal = lax.broadcasted_iota(jnp.int32, (width, width), 0) == lax.broadcasted_iota(
        jnp.int32, (width, width), 1
    )

    def set_weights(b, s, value):
        value = value.astype(jnp.bfloat16)
        if (b, s) == (0, 0):
            w_low[...] = value
        elif (b, s) == (1, 2):
            w_high[...] = value
        else:
            c = b + s - 1
            w_own[b * width:(b + 1) * width, c * width:(c + 1) * width] = value

    pmv_copies[0].wait()
    for b in range(2):
        for s in range(3):
            set_weights(b, s, p[b, s])
    own_copy.wait()

    def run_pass(rows, size, fields_row, turn):
        x_own, x_low, x_high = own[rows, :], low[rows, :], high[rows, :]
        if turn:
            turned[:width, rows] = x_low.T
            turned[width:3 * width, rows] = x_own.T
            turned[3 * width:, rows] = x_high.T
        inner = dot(x_own, w_own[...])
        outer = jnp.concatenate([dot_nt(x_low, w_low[...]), dot_nt(x_high, w_high[...])], axis=1)
        logits = inner + outer + fields_row
        deviation = 0.5 * jnp.tanh(0.5 * logits) + (0.5 - x_own.astype(jnp.float32))
        field_sum[...] += jnp.sum(deviation.reshape(size // 8, 8, 2 * width), axis=0)
        residual = deviation.astype(jnp.bfloat16)
        half_low[...] += dot(turned[:3 * width, rows], residual[:, :width])
        half_high[...] += dot(turned[width:, rows], residual[:, width:])

    def gradient_of(step, b, s):
        if (b, s) == (0, 0):
            value = half_low[:width, :].T + mirror_recv[step, 1].astype(jnp.float32)
        elif (b, s) == (1, 2):
            value = half_high[2 * width:, :].T + mirror_recv[step, 0].astype(jnp.float32)
        elif s == 1:
            half = half_low[width:2 * width, :] if b == 0 else half_high[width:2 * width, :]
            value = jnp.where(diagonal, 0.0, half + half.T)
        elif b == 0:
            value = half_high[:width, :] + half_low[2 * width:, :].T
        else:
            value = half_low[2 * width:, :] + half_high[:width, :].T
        return value * pattern[b, s].astype(jnp.float32)

    for step in range(2):
        half_low[...] = jnp.zeros_like(half_low)
        half_high[...] = jnp.zeros_like(half_high)
        field_sum[...] = jnp.zeros_like(field_sum)
        if step == 0:
            @pl.loop(0, pieces)
            def _(i):
                @pl.when(has_left)
                def _():
                    halo_copy(1, i).wait_recv()

                @pl.when(has_right)
                def _():
                    halo_copy(0, i).wait_recv()

                run_pass(pl.ds(pl.multiple_of(i * PIECE, PIECE), PIECE), PIECE, fields[...], True)
        else:
            @pl.loop(0, frame_count // SPAN)
            def _(i):
                run_pass(pl.ds(pl.multiple_of(i * SPAN, SPAN), SPAN), SPAN, fields_out[...], False)

        mirror_send[step, 0] = half_low[:width, :].astype(jnp.bfloat16)
        mirror_send[step, 1] = half_high[2 * width:, :].astype(jnp.bfloat16)

        @pl.when(has_left)
        def _():
            mirror_copy(step, 0).start()

        @pl.when(has_right)
        def _():
            mirror_copy(step, 1).start()

        field_grad = jnp.sum(field_sum[...], axis=0, keepdims=True)
        if step == 0:
            fields_out[...], field_first_out[...], field_second_out[...] = adam_update(
                fields[...], field_first[...], field_second[...], field_grad, PRIOR_STEPS + 1
            )
            pmv_copies[1].wait()
            pmv_copies[2].wait()
        else:
            field_grad_out[...] = field_grad

        for b, s in ((0, 1), (0, 2), (1, 0), (1, 1), (0, 0), (1, 2)):
            if (b, s) == (0, 0):
                @pl.when(has_left)
                def _():
                    mirror_copy(step, 1).wait_recv()
            elif (b, s) == (1, 2):
                @pl.when(has_right)
                def _():
                    mirror_copy(step, 0).wait_recv()
            gradient = gradient_of(step, b, s)
            if step == 0:
                p[b, s], m[b, s], v[b, s] = adam_update(
                    p[b, s], m[b, s], v[b, s], gradient, PRIOR_STEPS + 1
                )
                set_weights(b, s, p[b, s])
            else:
                grad_out[b, s] = gradient
        if step == 0:
            out_copies = [
                pltpu.make_async_copy(src, dst, out_sem.at[k])
                for k, (src, dst) in enumerate(((p, p_out), (m, m_out), (v, v_out)))
            ]
            for c in out_copies:
                c.start()

    for c in out_copies:
        c.wait()

    @pl.when(has_left)
    def _():
        for step in range(2):
            mirror_copy(step, 0).wait_send()

    @pl.when(has_right)
    def _():
        for step in range(2):
            mirror_copy(step, 1).wait_send()

    @pl.loop(0, pieces)
    def _(i):
        @pl.when(has_left)
        def _():
            halo_copy(0, i).wait_send()

        @pl.when(has_right)
        def _():
            halo_copy(1, i).wait_send()


def on_device(
    count, frames, pattern, couplings, first_moment, second_moment, fields, field_first, field_second
):
    frame_count, neurons = frames.shape
    width = couplings.shape[-1]
    blocks = jax.ShapeDtypeStruct(couplings.shape, jnp.float32)
    row = jax.ShapeDtypeStruct((1, neurons), jnp.float32)
    vmem = pl.BlockSpec(memory_space=pltpu.VMEM)
    anywhere = pl.BlockSpec(memory_space=pl.ANY)
    pieces = frame_count // PIECE
    p, m, v, gradient, f, ff, fs, field_grad = pl.pallas_call(
        functools.partial(kernel, count),
        out_shape=[blocks, blocks, blocks, blocks, row, row, row, row],
        in_specs=[anywhere, pl.BlockSpec(memory_space=pltpu.SMEM)] + [anywhere] * 3 + [vmem] * 3,
        out_specs=[anywhere] * 3 + [vmem] * 5,
        scratch_shapes=[
            pltpu.VMEM((frame_count, neurons), jnp.bfloat16),
            pltpu.VMEM((frame_count, width), jnp.bfloat16),
            pltpu.VMEM((frame_count, width), jnp.bfloat16),
            pltpu.VMEM((4 * width, frame_count), jnp.bfloat16),
            pltpu.VMEM(couplings.shape, jnp.float32),
            pltpu.VMEM(couplings.shape, jnp.float32),
            pltpu.VMEM(couplings.shape, jnp.float32),
            pltpu.VMEM((neurons, neurons), jnp.bfloat16),
            pltpu.VMEM((width, width), jnp.bfloat16),
            pltpu.VMEM((width, width), jnp.bfloat16),
            pltpu.VMEM((3 * width, width), jnp.float32),
            pltpu.VMEM((3 * width, width), jnp.float32),
            pltpu.VMEM((8, neurons), jnp.float32),
            pltpu.VMEM((2, 2, width, width), jnp.bfloat16),
            pltpu.VMEM((2, 2, width, width), jnp.bfloat16),
            pltpu.SemaphoreType.DMA((2, pieces)),
            pltpu.SemaphoreType.DMA((2, pieces)),
            pltpu.SemaphoreType.DMA((2, 2)),
            pltpu.SemaphoreType.DMA((2, 2)),
            pltpu.SemaphoreType.DMA,
            pltpu.SemaphoreType.DMA((3,)),
            pltpu.SemaphoreType.DMA((3,)),
        ],
        compiler_params=pltpu.CompilerParams(
            collective_id=0, has_side_effects=True, vmem_limit_bytes=48 * 1024 * 1024
        ),
    )(
        frames, pattern, couplings, first_moment, second_moment,
        fields.reshape(1, neurons), field_first.reshape(1, neurons), field_second.reshape(1, neurons),
    )
    p, m, v = adam_update(p, m, v, gradient, PRIOR_STEPS + 2)
    f, ff, fs = adam_update(
        f.reshape(neurons), ff.reshape(neurons), fs.reshape(neurons),
        field_grad.reshape(neurons), PRIOR_STEPS + 2,
    )
    return (p, m, v, f, ff, fs)


def solution(mesh):
    blocks = P(("grp", "row"), None, None, None)
    vector = P(("grp", "row"))
    return jax.shard_map(
        functools.partial(on_device, mesh.shape["row"]),
        mesh=mesh,
        in_specs=(P("grp", "row"), P(("grp", "row"), None)) + (blocks,) * 3 + (vector,) * 3,
        out_specs=(blocks,) * 3 + (vector,) * 3,
        check_vma=False,
    )
```

time: 224 us -> 51.7 us (0.23)
  waiting for transfers between devices: 83.3 us -> 0 us
  local copies, waits for them, and re-layouts: 48.8 us -> 2.72 us
  Pallas kernels: 0 us -> 42.9 us
  starting transfers between devices: 37.6 us -> 0 us
  other arithmetic: 36.9 us -> 4.77 us
  matrix products: 14.4 us -> 0 us
    ppermute x12 -> x0, waiting for transfers between devices: 83.3 us -> none  [the longest x6 83.3 us: with_halo(): lax.ppermute(lax.slice_in_dim(block, block.shape[dim] - width, None, axis...]
    pallas_call x0 -> x1, Pallas kernels: none -> 42.9 us  [on_device(): pl.pallas_call(functools.partial(kernel, count), out_shape=[blocks, block...]
    ppermute x12 -> x0, starting transfers between devices: 37.6 us -> none  [the longest x6 25.9 us: with_halo(): lax.ppermute(lax.slice_in_dim(block, block.shape[dim] - width, None, axis...]
    concatenate x4 -> x0, local copies, waits for them, and re-layouts: 14.6 us -> none  [with_halo(): block = jnp.concatenate([low, block, high], axis=dim)]
    dot_general x6 -> x0, matrix products: 14.4 us -> none  [the longest x4 8.54 us: on_device(): jnp.einsum('fb,fsc->sbc', spikes[:, local_row], windows[:, local_row:loca...]
    div x2 -> x0, local copies, waits for them, and re-layouts: 11 us -> none  [on_device(): deviation = jax.nn.sigmoid(logits) - spikes_float]
    another operation x9 -> x0, other arithmetic: 9 us -> none  [the longest x4 7.36 us: on_device(): jnp.stack([halves[0, 0] + mirror_below.T, halves[0, 1] + halves[0, 1].T,...]
    squeeze x9 -> x0, local copies, waits for them, and re-layouts: 7.66 us -> none  [the longest x2 2.51 us: on_device(): halves[1, 0]]
  transfers between devices with their start and end apart: 12 -> 0, of which waited for: 4 -> 0; matrix products, arithmetic and copies ran while one was open for 5% -> 0% of each run, Pallas kernels for 0% -> 0%
where the time goes in v1:
time: 51.7 us; the launch traced here: 51.1 us
  Pallas kernels  42.9 us (83%)
  other arithmetic  4.77 us (9%)
  local copies, waits for them, and re-layouts  2.72 us (5%)
  between operations  0.66 us (1%)
    pallas_call x1, Pallas kernels, on_device(): pl.pallas_call(functools.partial(kernel, count), out_shape=[blocks, block...  42.9 us
    sub x2, other arithmetic, adam_update(): parameter - first_rate * first_moment / (jnp.sqrt(second_hat) + EPSILON)  4.77 us
    unnamed x8, local copies, waits for them, and re-layouts  2.72 us

profile of v1, /device:TPU:1, one launch (start us, length us, event | category | flops | bytes accessed | tf_op | source)
XLA Modules:
  0.0 51.1 jit_solution(14901213867651181207)
XLA Ops:
  0.6 0.0 copy-start
  0.6 0.7 %copy-done = f32[512]{0:T(512)S(1)} copy-done((f32[512]{0:T(512)S(1)}, f32[512]{0:T(512)}, u32[]{:S(2)}) %copy-start) | copy-done | bytes 2072
  1.3 0.0 copy-start.1
  1.3 0.7 %copy-done.1 = f32[512]{0:T(512)S(1)} copy-done((f32[512]{0:T(512)S(1)}, f32[512]{0:T(512)}, u32[]{:S(2)}) %copy-start.1) | copy-done | bytes 2072
  2.0 0.0 copy-start.2
  2.0 0.7 %copy-done.2 = f32[512]{0:T(512)S(1)} copy-done((f32[512]{0:T(512)S(1)}, f32[512]{0:T(512)}, u32[]{:S(2)}) %copy-start.2) | copy-done | bytes 2072
  2.7 0.0 copy-start.3
  2.7 0.7 %copy-done.3 = s32[2,3]{1,0:T(2,128)S(1)} copy-done((s32[2,3]{1,0:T(2,128)S(1)}, s32[2,3]{1,0:T(2,128)}, u32[]{:S(2)}) %copy-start.3) | copy-done | bytes 48
  3.4 42.9 %shard_map.127 = (f32[2,3,256,256]{3,2,1,0:T(8,128)S(1)}, f32[2,3,256,256]{3,2,1,0:T(8,128)S(1)}, f32[2,3,256,256]{3,2,1,0:T(8,128)S(1)}, f32[2,3,256,256]{3,2,1...) custom-call(bf16[2048,512]{1,0:T(8,128)(2,1)} %frames_hbm.1, ...), custom_call_target="tpu_custom_call" | custom-call | tf_op jit(solution)/shard_map/pallas_call | solution.py:267
  46.3 0.6 %divide_subtract_fusion.1 = (f32[512]{0:T(512)}, f32[512]{0:T(512)}, f32[512]{0:T(512)}) fusion(f32[512]{0:T(512)S(1)} %bitcast.10, f32[512]{0:T(512)S(1)} %bitcast.13, f32[512]{0:T(512)S(1)} %bitcast.11, f32[512]{0:T(512)S(1)} %bitcast.12), kind=kLoop, calls=%fused_computation.6 | loop fusion | flops 5120 | bytes 14336 | tf_op jit(solution)/shard_map/sub | solution.py:25
  46.9 4.2 %divide_subtract_fusion = (f32[2,3,256,256]{3,2,1,0:T(8,128)}, f32[2,3,256,256]{3,2,1,0:T(8,128)}, f32[2,3,256,256]{3,2,1,0:T(8,128)}) fusion(f32[2,3,256,256]{3,2,1,0:T(8,128)S(1)} %get-tuple-element.14, f32[2,3,256,256]{3,2,1,0:T(8,128)} %get-tuple-element.16, f32[2,3,256,256]{3,2,1,0:T(8,128)S(1)} %get-tuple-element.15, ...), kind=kLoop, calls=%fused_computation.2 | loop fusion | flops 4718592 | bytes 11010048 | tf_op jit(solution)/shard_map/sub | solution.py:25
  (1 shorter events, 0.0 us)
Async XLA Ops:
  0.6 0.7 %copy-start = (f32[512]{0:T(512)S(1)}, f32[512]{0:T(512)}, u32[]{:S(2)}) copy-start(f32[512]{0:T(512)} %param.13) | copy-start | bytes 6148
  1.3 0.7 %copy-start.1 = (f32[512]{0:T(512)S(1)}, f32[512]{0:T(512)}, u32[]{:S(2)}) copy-start(f32[512]{0:T(512)} %param.14) | copy-start | bytes 6148
  2.0 0.7 %copy-start.2 = (f32[512]{0:T(512)S(1)}, f32[512]{0:T(512)}, u32[]{:S(2)}) copy-start(f32[512]{0:T(512)} %param.15) | copy-start | bytes 6148
  2.7 0.7 %copy-start.3 = (s32[2,3]{1,0:T(2,128)S(1)}, s32[2,3]{1,0:T(2,128)}, u32[]{:S(2)}) copy-start(s32[2,3]{1,0:T(2,128)} %pattern.1) | copy-start | bytes 76

commit v2 on v1

--- a/solution.py
+++ b/solution.py
@@ -36,11 +36,10 @@
 
 def kernel(
     count,
-    frames_hbm, pattern, p_hbm, m_hbm, v_hbm, fields, field_first, field_second,
-    p_out, m_out, v_out, grad_out, fields_out, field_first_out, field_second_out, field_grad_out,
-    own, low, high, turned, p, m, v, w_own, w_low, w_high, half_low, half_high, field_sum,
-    mirror_send, mirror_recv,
-    halo_send_sem, halo_recv_sem, mirror_send_sem, mirror_recv_sem, own_sem, pmv_sem, out_sem,
+    frames_hbm, p_hbm, m_hbm, v_hbm, vectors, p_out, m_out, v_out, vectors_out,
+    own, low, high, turned, residuals, p, m, v, w_own, w_low, w_high, half_low, half_high, local,
+    field_sum, fields, mirror_send, mirror_recv,
+    halo_send_sem, halo_recv_sem, mirror_send_sem, mirror_recv_sem, own_sem, load_sem, out_sem,
 ):
     frame_count, width = low.shape
     pieces = frame_count // PIECE
@@ -51,12 +50,12 @@
     has_right = me < count - 1
 
     own_copy = pltpu.make_async_copy(frames_hbm, own, own_sem)
-    pmv_copies = [
-        pltpu.make_async_copy(src, dst, pmv_sem.at[k])
+    loads = [
+        pltpu.make_async_copy(src, dst, load_sem.at[k])
         for k, (src, dst) in enumerate(((p_hbm, p), (m_hbm, m), (v_hbm, v)))
     ]
     own_copy.start()
-    for c in pmv_copies:
+    for c in loads:
         c.start()
 
     def halo_copy(flow, i):
@@ -128,13 +127,14 @@
             c = b + s - 1
             w_own[b * width:(b + 1) * width, c * width:(c + 1) * width] = value
 
-    pmv_copies[0].wait()
+    fields[...] = vectors[:1, :]
+    loads[0].wait()
     for b in range(2):
         for s in range(3):
             set_weights(b, s, p[b, s])
     own_copy.wait()
 
-    def run_pass(rows, size, fields_row, turn):
+    def run_pass(rows, size, turn):
         x_own, x_low, x_high = own[rows, :], low[rows, :], high[rows, :]
         if turn:
             turned[:width, rows] = x_low.T
@@ -142,27 +142,29 @@
             turned[3 * width:, rows] = x_high.T
         inner = dot(x_own, w_own[...])
         outer = jnp.concatenate([dot_nt(x_low, w_low[...]), dot_nt(x_high, w_high[...])], axis=1)
-        logits = inner + outer + fields_row
+        logits = inner + outer + fields[...]
         deviation = 0.5 * jnp.tanh(0.5 * logits) + (0.5 - x_own.astype(jnp.float32))
         field_sum[...] += jnp.sum(deviation.reshape(size // 8, 8, 2 * width), axis=0)
         residual = deviation.astype(jnp.bfloat16)
-        half_low[...] += dot(turned[:3 * width, rows], residual[:, :width])
-        half_high[...] += dot(turned[width:, rows], residual[:, width:])
+        residuals[rows, :] = residual
+        half_low[...] += dot(turned[:width, rows], residual[:, :width])
+        half_high[...] += dot(turned[3 * width:, rows], residual[:, width:])
 
     def gradient_of(step, b, s):
         if (b, s) == (0, 0):
-            value = half_low[:width, :].T + mirror_recv[step, 1].astype(jnp.float32)
+            value = half_low[...].T + mirror_recv[step, 1].astype(jnp.float32)
         elif (b, s) == (1, 2):
-            value = half_high[2 * width:, :].T + mirror_recv[step, 0].astype(jnp.float32)
-        elif s == 1:
-            half = half_low[width:2 * width, :] if b == 0 else half_high[width:2 * width, :]
-            value = jnp.where(diagonal, 0.0, half + half.T)
-        elif b == 0:
-            value = half_high[:width, :] + half_low[2 * width:, :].T
+            value = half_high[...].T + mirror_recv[step, 0].astype(jnp.float32)
         else:
-            value = half_low[2 * width:, :] + half_high[:width, :].T
-        return value * pattern[b, s].astype(jnp.float32)
-
+            one = slice(b * width, (b + 1) * width)
+            two = slice((b + s - 1) * width, (b + s) * width)
+            value = local[one, two] + local[two, one].T
+            if s == 1:
+                value = jnp.where(diagonal, 0.0, value)
+        slot = 3 * b + s
+        return value * vectors[3:4, slot:slot + 1]
+
+    out_copies = []
     for step in range(2):
         half_low[...] = jnp.zeros_like(half_low)
         half_high[...] = jnp.zeros_like(half_high)
@@ -178,14 +180,14 @@
                 def _():
                     halo_copy(0, i).wait_recv()
 
-                run_pass(pl.ds(pl.multiple_of(i * PIECE, PIECE), PIECE), PIECE, fields[...], True)
+                run_pass(pl.ds(pl.multiple_of(i * PIECE, PIECE), PIECE), PIECE, True)
         else:
             @pl.loop(0, frame_count // SPAN)
             def _(i):
-                run_pass(pl.ds(pl.multiple_of(i * SPAN, SPAN), SPAN), SPAN, fields_out[...], False)
-
-        mirror_send[step, 0] = half_low[:width, :].astype(jnp.bfloat16)
-        mirror_send[step, 1] = half_high[2 * width:, :].astype(jnp.bfloat16)
+                run_pass(pl.ds(pl.multiple_of(i * SPAN, SPAN), SPAN), SPAN, False)
+
+        mirror_send[step, 0] = half_low[...].astype(jnp.bfloat16)
+        mirror_send[step, 1] = half_high[...].astype(jnp.bfloat16)
 
         @pl.when(has_left)
         def _():
@@ -195,15 +197,18 @@
         def _():
             mirror_copy(step, 1).start()
 
+        if step == 0:
+            for c in loads[1:]:
+                c.wait()
         field_grad = jnp.sum(field_sum[...], axis=0, keepdims=True)
         if step == 0:
-            fields_out[...], field_first_out[...], field_second_out[...] = adam_update(
-                fields[...], field_first[...], field_second[...], field_grad, PRIOR_STEPS + 1
+            fields[...], vectors_out[1:2, :], vectors_out[2:3, :] = adam_update(
+                fields[...], vectors[1:2, :], vectors[2:3, :], field_grad, PRIOR_STEPS + 1
             )
-            pmv_copies[1].wait()
-            pmv_copies[2].wait()
+            vectors_out[:1, :] = fields[...]
         else:
-            field_grad_out[...] = field_grad
+            vectors_out[3:4, :] = field_grad
+        local[...] = dot(turned[width:3 * width, :], residuals[...])
 
         for b, s in ((0, 1), (0, 2), (1, 0), (1, 1), (0, 0), (1, 2)):
             if (b, s) == (0, 0):
@@ -214,21 +219,16 @@
                 @pl.when(has_right)
                 def _():
                     mirror_copy(step, 0).wait_recv()
-            gradient = gradient_of(step, b, s)
+            p[b, s], m[b, s], v[b, s] = adam_update(
+                p[b, s], m[b, s], v[b, s], gradient_of(step, b, s), PRIOR_STEPS + 1 + step
+            )
             if step == 0:
-                p[b, s], m[b, s], v[b, s] = adam_update(
-                    p[b, s], m[b, s], v[b, s], gradient, PRIOR_STEPS + 1
-                )
                 set_weights(b, s, p[b, s])
             else:
-                grad_out[b, s] = gradient
-        if step == 0:
-            out_copies = [
-                pltpu.make_async_copy(src, dst, out_sem.at[k])
-                for k, (src, dst) in enumerate(((p, p_out), (m, m_out), (v, v_out)))
-            ]
-            for c in out_copies:
-                c.start()
+                for k, (src, dst) in enumerate(((p, p_out), (m, m_out), (v, v_out))):
+                    copy = pltpu.make_async_copy(src.at[b, s], dst.at[b, s], out_sem.at[k, 3 * b + s])
+                    copy.start()
+                    out_copies.append(copy)
 
     for c in out_copies:
         c.wait()
@@ -260,29 +260,38 @@
     frame_count, neurons = frames.shape
     width = couplings.shape[-1]
     blocks = jax.ShapeDtypeStruct(couplings.shape, jnp.float32)
-    row = jax.ShapeDtypeStruct((1, neurons), jnp.float32)
+    rows = jax.ShapeDtypeStruct((4, neurons), jnp.float32)
     vmem = pl.BlockSpec(memory_space=pltpu.VMEM)
     anywhere = pl.BlockSpec(memory_space=pl.ANY)
     pieces = frame_count // PIECE
-    p, m, v, gradient, f, ff, fs, field_grad = pl.pallas_call(
+    vectors = jnp.stack(
+        [
+            fields, field_first, field_second,
+            jnp.pad(pattern.reshape(-1).astype(jnp.float32), (0, neurons - pattern.size)),
+        ]
+    )
+    p, m, v, vectors = pl.pallas_call(
         functools.partial(kernel, count),
-        out_shape=[blocks, blocks, blocks, blocks, row, row, row, row],
-        in_specs=[anywhere, pl.BlockSpec(memory_space=pltpu.SMEM)] + [anywhere] * 3 + [vmem] * 3,
-        out_specs=[anywhere] * 3 + [vmem] * 5,
+        out_shape=[blocks, blocks, blocks, rows],
+        in_specs=[anywhere] * 4 + [vmem],
+        out_specs=[anywhere] * 3 + [vmem],
         scratch_shapes=[
             pltpu.VMEM((frame_count, neurons), jnp.bfloat16),
             pltpu.VMEM((frame_count, width), jnp.bfloat16),
             pltpu.VMEM((frame_count, width), jnp.bfloat16),
             pltpu.VMEM((4 * width, frame_count), jnp.bfloat16),
+            pltpu.VMEM((frame_count, neurons), jnp.bfloat16),
             pltpu.VMEM(couplings.shape, jnp.float32),
             pltpu.VMEM(couplings.shape, jnp.float32),
             pltpu.VMEM(couplings.shape, jnp.float32),
             pltpu.VMEM((neurons, neurons), jnp.bfloat16),
             pltpu.VMEM((width, width), jnp.bfloat16),
             pltpu.VMEM((width, width), jnp.bfloat16),
-            pltpu.VMEM((3 * width, width), jnp.float32),
-            pltpu.VMEM((3 * width, width), jnp.float32),
+            pltpu.VMEM((width, width), jnp.float32),
+            pltpu.VMEM((width, width), jnp.float32),
+            pltpu.VMEM((neurons, neurons), jnp.float32),
             pltpu.VMEM((8, neurons), jnp.float32),
+            pltpu.VMEM((1, neurons), jnp.float32),
             pltpu.VMEM((2, 2, width, width), jnp.bfloat16),
             pltpu.VMEM((2, 2, width, width), jnp.bfloat16),
             pltpu.SemaphoreType.DMA((2, pieces)),
@@ -291,20 +300,15 @@
             pltpu.SemaphoreType.DMA((2, 2)),
             pltpu.SemaphoreType.DMA,
             pltpu.SemaphoreType.DMA((3,)),
-            pltpu.SemaphoreType.DMA((3,)),
+            pltpu.SemaphoreType.DMA((3, 6)),
         ],
         compiler_params=pltpu.CompilerParams(
             collective_id=0, has_side_effects=True, vmem_limit_bytes=48 * 1024 * 1024
         ),
     )(
-        frames, pattern, couplings, first_moment, second_moment,
-        fields.reshape(1, neurons), field_first.reshape(1, neurons), field_second.reshape(1, neurons),
+        frames, couplings, first_moment, second_moment, vectors
     )
-    p, m, v = adam_update(p, m, v, gradient, PRIOR_STEPS + 2)
-    f, ff, fs = adam_update(
-        f.reshape(neurons), ff.reshape(neurons), fs.reshape(neurons),
-        field_grad.reshape(neurons), PRIOR_STEPS + 2,
-    )
+    f, ff, fs = adam_update(vectors[0], vectors[1], vectors[2], vectors[3], PRIOR_STEPS + 2)
     return (p, m, v, f, ff, fs)
 
 

time: 51.7 us -> 47.6 us (0.921)
  other arithmetic: 4.77 us -> 2.02 us
  Pallas kernels: 42.9 us -> 41.2 us
  local copies, waits for them, and re-layouts: 2.72 us -> 3.52 us
    sub x2 -> x1, other arithmetic: 4.77 us -> 0.6 us  [adam_update(): parameter - first_rate * first_moment / (jnp.sqrt(second_hat) + EPSILON)]
    pallas_call x1, Pallas kernels: 42.9 us -> 41.2 us  [on_device(): pl.pallas_call(functools.partial(kernel, count), out_shape=[blocks, block...]
    another operation x0 -> x1, other arithmetic: none -> 0.73 us  [on_device(): jnp.stack([fields, field_first, field_second, jnp.pad(pattern.reshape(-1)...]
    unnamed x8 -> x3, local copies, waits for them, and re-layouts: 2.72 us -> 3.43 us
    convert_element_type x0 -> x1, other arithmetic: none -> 0.68 us  [on_device(): pattern.reshape(-1).astype(jnp.float32)]
where the time goes in v2:
time: 47.6 us; the launch traced here: 47.4 us
  Pallas kernels  41.2 us (87%)
  local copies, waits for them, and re-layouts  3.52 us (7%)
  other arithmetic  2.02 us (4%)
  between operations  0.65 us (1%)
    pallas_call x1, Pallas kernels, on_device(): pl.pallas_call(functools.partial(kernel, count), out_shape=[blocks, block...  41.2 us
    unnamed x3, local copies, waits for them, and re-layouts  3.43 us

profile of v2, /device:TPU:1, one launch (start us, length us, event | category | flops | bytes accessed | tf_op | source)
XLA Modules:
  0.0 47.4 jit_solution(12513717582498058224)
XLA Ops:
  0.6 0.7 %convert_element_type.8 = f32[2,3]{1,0:T(2,128)S(1)} convert(s32[2,3]{1,0:T(2,128)} %param.9) | non-fusion elementwise | flops 6 | bytes 48 | tf_op jit(solution)/shard_map/convert_element_type | solution.py:270
  1.3 0.1 convert_element_type.9
  1.4 0.7 %pad_maximum_fusion.vectors = f32[4,512]{1,0:T(4,128)S(1)} fusion(f32[1,512]{1,0:T(1,128)S(1)} %bitcast.12, f32[1,512]{1,0:T(1,128)} %bitcast.13, f32[1,512]{1,0:T(1,128)} %bitcast.14, f32[1,512]{1,0:T(1,128)} %bitcast.15), kind=kLoop, calls=%fused_computation | loop fusion | flops 6144 | bytes 16384 | tf_op jit(solution)/shard_map/stack | solution.py:267
  2.1 41.2 %shard_map.127 = (f32[2,3,256,256]{3,2,1,0:T(8,128)S(1)}, f32[2,3,256,256]{3,2,1,0:T(8,128)S(1)}, f32[2,3,256,256]{3,2,1,0:T(8,128)S(1)}, f32[4,512]{1,0:T(4,128)S(1)}) custom-call(bf16[2048,512]{1,0:T(8,128)(2,1)} %frames_hbm.1, f32[2,3,256,256]{3,2,1,0:T(8,128)} %p_hbm.1, f32[2,3,256,256]{3,2,1,0:T(8,128)} %m_hbm.1, f32[2,3,256,256]{3,2,1,0:T(8,128)} %v_hbm.1, ...), custom_call_target="tpu_custom_call" | custom-call | tf_op jit(solution)/shard_map/pallas_call | solution.py:273
  43.4 0.6 %divide_subtract_fusion = (f32[512]{0:T(512)}, f32[512]{0:T(512)}, f32[512]{0:T(512)}) fusion(f32[512]{0:T(512)S(1)} %bitcast.11, f32[512]{0:T(512)S(1)} %bitcast.10, f32[512]{0:T(512)S(1)} %bitcast.9, f32[512]{0:T(512)S(1)} %bitcast.8), kind=kLoop, calls=%fused_computation.3 | loop fusion | flops 5120 | bytes 14336 | tf_op jit(solution)/shard_map/sub | solution.py:25
  44.0 1.1 %copy.17 = f32[2,3,256,256]{3,2,1,0:T(8,128)} copy(f32[2,3,256,256]{3,2,1,0:T(8,128)S(1)} %get-tuple-element.27) | data formatting | bytes 3145728
  45.1 1.1 %copy.18 = f32[2,3,256,256]{3,2,1,0:T(8,128)} copy(f32[2,3,256,256]{3,2,1,0:T(8,128)S(1)} %get-tuple-element.28) | data formatting | bytes 3145728
  46.3 1.1 %copy.19 = f32[2,3,256,256]{3,2,1,0:T(8,128)} copy(f32[2,3,256,256]{3,2,1,0:T(8,128)S(1)} %get-tuple-element.29) | data formatting | bytes 3145728
  (2 shorter events, 0.0 us)

commit v3 on v2

--- a/solution.py
+++ b/solution.py
@@ -161,8 +161,7 @@
             value = local[one, two] + local[two, one].T
             if s == 1:
                 value = jnp.where(diagonal, 0.0, value)
-        slot = 3 * b + s
-        return value * vectors[3:4, slot:slot + 1]
+        return value * vectors[3 + b:4 + b, s:s + 1]
 
     out_copies = []
     for step in range(2):
@@ -254,6 +253,18 @@
             halo_copy(1, i).wait_send()
 
 
+def store_kernel(p, m, v, p_out, m_out, v_out, sem):
+    copies = [
+        pltpu.make_async_copy(src.at[b], dst.at[b], sem.at[k, b])
+        for k, (src, dst) in enumerate(((p, p_out), (m, m_out), (v, v_out)))
+        for b in range(2)
+    ]
+    for c in copies:
+        c.start()
+    for c in copies:
+        c.wait()
+
+
 def on_device(
     count, frames, pattern, couplings, first_moment, second_moment, fields, field_first, field_second
 ):
@@ -264,10 +275,10 @@
     vmem = pl.BlockSpec(memory_space=pltpu.VMEM)
     anywhere = pl.BlockSpec(memory_space=pl.ANY)
     pieces = frame_count // PIECE
-    vectors = jnp.stack(
+    vectors = jnp.concatenate(
         [
-            fields, field_first, field_second,
-            jnp.pad(pattern.reshape(-1).astype(jnp.float32), (0, neurons - pattern.size)),
+            fields[None], field_first[None], field_second[None],
+            jnp.pad(pattern.astype(jnp.float32), ((0, 0), (0, neurons - pattern.shape[1]))),
         ]
     )
     p, m, v, vectors = pl.pallas_call(
@@ -308,6 +319,13 @@
     )(
         frames, couplings, first_moment, second_moment, vectors
     )
+    p, m, v = pl.pallas_call(
+        store_kernel,
+        out_shape=[blocks] * 3,
+        in_specs=[anywhere] * 3,
+        out_specs=[anywhere] * 3,
+        scratch_shapes=[pltpu.SemaphoreType.DMA((3, 2))],
+    )(p, m, v)
     f, ff, fs = adam_update(vectors[0], vectors[1], vectors[2], vectors[3], PRIOR_STEPS + 2)
     return (p, m, v, f, ff, fs)
 

time: 47.6 us -> 193 us (4.05)
  Pallas kernels: 41.2 us -> 186 us
    pallas_call x0 -> x1, Pallas kernels: none -> 144 us  [on_device(): pl.pallas_call(store_kernel, out_shape=[blocks] * 3, in_specs=[anywhere]...]
where the time goes in v3:
time: 193 us
  Pallas kernels  186 us (96%)
  local copies, waits for them, and re-layouts  3.46 us (2%)
  other arithmetic  2.02 us (1%)
    pallas_call x1, Pallas kernels, on_device(): pl.pallas_call(store_kernel, out_shape=[blocks] * 3, in_specs=[anywhere]...  144 us
    pallas_call x1, Pallas kernels, on_device(): pl.pallas_call(functools.partial(kernel, count), out_shape=[blocks, block...  42.3 us

profile of v3, /device:TPU:1, one launch (start us, length us, event | category | flops | bytes accessed | tf_op | source)
XLA Modules:
  0.0 192.6 jit_solution(11714940346965038073)
XLA Ops:
  0.6 0.7 convert_element_type.5
  1.3 0.7 select_maximum_fusion.vectors
  2.0 42.3 %shard_map.127 = (f32[2,3,256,256]{3,2,1,0:T(8,128)S(1)}, f32[2,3,256,256]{3,2,1,0:T(8,128)S(1)}, f32[2,3,256,256]{3,2,1,0:T(8,128)S(1)}, f32[4,512]{1,0:T(4,128)S(1)}) custom-call(bf16[2048,512]{1,0:T(8,128)(2,1)} %frames_hbm.1, f32[2,3,256,256]{3,2,1,0:T(8,128)} %p_hbm.1, f32[2,3,256,256]{3,2,1,0:T(8,128)} %m_hbm.1, f32[2,3,256,256]{3,2,1,0:T(8,128)} %v_hbm.1, ...), custom_call_target="tpu_custom_call" | custom-call | tf_op jit(solution)/shard_map/pallas_call | solution.py:284
  44.4 0.0 copy-start
  44.4 1.1 copy-done
  45.5 0.0 copy-start.1
  45.5 1.2 copy-done.1
  46.7 0.0 copy-start.2
  46.7 1.2 copy-done.2
  47.9 0.6 divide_subtract_fusion
  48.5 144.1 %shard_map.128 = (f32[2,3,256,256]{3,2,1,0:T(8,128)}, f32[2,3,256,256]{3,2,1,0:T(8,128)}, f32[2,3,256,256]{3,2,1,0:T(8,128)}) custom-call(f32[2,3,256,256]{3,2,1,0:T(8,128)} %copy-done, f32[2,3,256,256]{3,2,1,0:T(8,128)} %copy-done.1, f32[2,3,256,256]{3,2,1,0:T(8,128)} %copy-done.2), custom_call_target="tpu_custom_call" | custom-call | tf_op jit(solution)/shard_map/pallas_call | solution.py:322
  (1 shorter events, 0.0 us)
Async XLA Ops:
  44.4 1.2 copy-start
  45.5 1.2 copy-start.1
  46.7 1.2 copy-start.2
